TPU v7x, 32 devices: a whole 2x2x4 slice. The times are simulated.
32 devices in a mesh: gx: 8 (over z, y), gz: 4 (over x, core).
Axes of the slice: x: 2, y: 2, z: 4, core: 2. Of those that a mesh axis runs over, the one named last changes fastest.
Arguments:
- whitened: float32 [2, 64, 1024, 512], P(None, 'gz', 'gx'), may hold values from -6 to 6
- observed: float32 [2, 1024, 512], P(None, 'gx'), may hold values from -12 to 12
- lower_x: bfloat16 [1024, 1024], P('gx'), as said below
- lower_y: bfloat16 [512, 512], P('gx'), as said below
- lower_z: bfloat16 [64, 64], replicated, as said below
- coupling_kernel: float32 [2, 3, 3, 3], replicated, may hold values from -1.25 to 1.25
Outputs:
- gradient: float32 [2, 64, 1024, 512], P(None, 'gz', 'gx')
- misfit: float32 [2, 1024, 512], P(None, 'gx')
Inputs may be any that keep to these rules, and one draw needn't show every extreme that they name: `lower_x`: lower triangular: zero above the diagonal, diagonal entries between 0.5 and 1.5. `lower_y`: lower triangular: zero above the diagonal, diagonal entries between 0.5 and 1.5. `lower_z`: lower triangular: zero above the diagonal, diagonal entries between 0.5 and 1.5.
All inputs are finite; a program needn't handle non-finite values.
Results may differ from a plain program's by a relative error of at most 0.013.
The roundings to bfloat16 on the way count: a program that leaves them out, or rounds other values in their place, can miss the bound.
Values may be sent and summed in bfloat16 or wider, within the bound.
A program may use at most 128 MiB of HBM per device.

v0:
```python
import math
import jax
import jax.numpy as jnp
from jax import lax
from jax.sharding import PartitionSpec as P

NZ = 64


def padded_2(x, sides, width):
    for axis, dim in sides:
        peers, length = (lax.axis_size(axis), x.shape[dim])
        up = [(i, (i + 1) % peers) for i in range(peers - 1)]
        down = [(j, i) for i, j in up]
        last = lax.slice_in_dim(x, length - width, length, axis=dim)
        first = lax.slice_in_dim(x, 0, width, axis=dim)
        before = lax.ppermute(last, axis, up)
        after = lax.ppermute(first, axis, down)
        x = jnp.concatenate([before, x, after], axis=dim)
    return x


def depth_lines(values, local_step):
    turned = lax.all_to_all(values, "gz", split_axis=3, concat_axis=1, tiled=True)
    return lax.all_to_all(local_step(turned), "gz", split_axis=1, concat_axis=3, tiled=True)


def across_lines(values, local_step):
    turned = lax.all_to_all(values, "gx", split_axis=3, concat_axis=2, tiled=True)
    return lax.all_to_all(local_step(turned), "gx", split_axis=2, concat_axis=3, tiled=True)


def stencil_sum(padded, kernel, depth_rows, x_rows, y_rows, flipped):
    total = jnp.zeros(padded.shape[:-3] + (depth_rows, x_rows, y_rows), jnp.float32)
    for offset_z in range(3):
        for offset_x in range(3):
            for offset_y in range(3):
                start_z = 2 - offset_z if flipped else offset_z
                start_x = 2 - offset_x if flipped else offset_x
                start_y = 2 - offset_y if flipped else offset_y
                total = (
                    total
                    + kernel[offset_z, offset_x, offset_y]
                    * padded[
                        ...,
                        start_z : start_z + depth_rows,
                        start_x : start_x + x_rows,
                        start_y : start_y + y_rows,
                    ]
                )
    return total


def depth_weights(first_row, depth_rows):
    depth = (first_row + jnp.arange(depth_rows)).astype(jnp.float32)
    factor = 4.0 / math.sqrt(NZ)
    return (factor / (1.0 + depth / NZ) ** 2, factor / (1.0 + depth / NZ) ** 3)


def coupling_forward(rim, magnetic_f, kernel, shape):
    depth_rows, x_rows, y_rows = shape
    pre_scale = stencil_sum(rim, kernel[0], depth_rows, x_rows, y_rows, False)
    pre_shift = stencil_sum(rim, kernel[1], depth_rows, x_rows, y_rows, False)
    scale = jnp.tanh(pre_scale)
    growth = jnp.exp(scale)
    return (scale, growth, magnetic_f * growth + pre_shift)


def local(whitened, observed, lower_x, lower_y, lower_z, coupling_kernel):
    factor_x, factor_y = (
        lax.all_gather(lower_x, "gx", axis=0, tiled=True),
        lax.all_gather(lower_y, "gx", axis=0, tiled=True),
    )

    def apply_depth(values):
        return jnp.einsum(
            "zk,fkxy->fzxy", lower_z, values, preferred_element_type=jnp.float32
        ).astype(jnp.bfloat16)

    def apply_across(values):
        return jnp.einsum(
            "xk,fzky->fzxy", factor_x, values, preferred_element_type=jnp.float32
        ).astype(jnp.bfloat16)

    def depth_adjoint(values):
        return jnp.einsum(
            "kz,fkxy->fzxy", lower_z, values, preferred_element_type=jnp.float32
        ).astype(jnp.bfloat16)

    def across_adjoint(values):
        return jnp.einsum(
            "kx,fzky->fzxy", factor_x, values, preferred_element_type=jnp.float32
        ).astype(jnp.bfloat16)

    start = whitened.astype(jnp.bfloat16)
    first = jnp.einsum("fzxk,yk->fzxy", start, factor_y, preferred_element_type=jnp.float32).astype(
        jnp.bfloat16
    )
    model = across_lines(depth_lines(first, apply_depth), apply_across)
    density = model[0]
    magnetic_f = model[1].astype(jnp.float32)
    depth_rows, x_rows, y_rows = density.shape
    rim = padded_2(density, (("gx", 1), ("gz", 0)), 1)
    rim = jnp.pad(rim, ((0, 0), (0, 0), (1, 1))).astype(jnp.float32)
    scale, growth, coupled = coupling_forward(
        rim, magnetic_f, coupling_kernel, (depth_rows, x_rows, y_rows)
    )
    weight_g, weight_m = depth_weights(lax.axis_index("gz") * depth_rows, depth_rows)
    part_g = jnp.einsum("z,zxy->xy", weight_g, density.astype(jnp.float32))
    part_m = jnp.einsum("z,zxy->xy", weight_m, coupled)
    predicted = lax.psum(jnp.stack([part_g, part_m]), "gz")
    misfit = predicted - observed
    back_g = weight_g[:, None, None] * misfit[0][None]
    back_m = weight_m[:, None, None] * misfit[1][None]
    back_scale = (back_m * magnetic_f * growth * (1.0 - scale * scale)).astype(jnp.bfloat16)
    back_shift = back_m.astype(jnp.bfloat16)
    cotangents = jnp.stack([back_scale, back_shift])
    outer = padded_2(cotangents, (("gx", 2), ("gz", 1)), 1)
    outer = jnp.pad(outer, ((0, 0), (0, 0), (0, 0), (1, 1))).astype(jnp.float32)
    spread_back = stencil_sum(outer[0], coupling_kernel[0], depth_rows, x_rows, y_rows, True)
    spread_back = spread_back + stencil_sum(
        outer[1], coupling_kernel[1], depth_rows, x_rows, y_rows, True
    )
    adjoint = jnp.stack([back_g + spread_back, back_m * growth]).astype(jnp.bfloat16)
    fourth = depth_lines(across_lines(adjoint, across_adjoint), depth_adjoint)
    gradient = whitened + jnp.einsum(
        "fzxk,ky->fzxy", fourth, factor_y, preferred_element_type=jnp.float32
    )
    return (gradient, misfit)


def solution(mesh):
    in_specs = (
        P(None, "gz", "gx", None),
        P(None, "gx", None),
        P("gx", None),
        P("gx", None),
        P(),
        P(),
    )
    out_specs = (P(None, "gz", "gx", None), P(None, "gx", None))
    return jax.shard_map(local, mesh=mesh, in_specs=in_specs, out_specs=out_specs, check_vma=False)
```

profile of v0, /device:TPU:0, one launch (start us, length us, event | category | flops | bytes accessed | tf_op | source)
XLA Modules:
  0.0 1367.9 jit_solution(581240853023325873)
XLA Ops:
  7.2 33.2 %all_gather.6 = bf16[512,512]{1,0:T(8,128)(2,1)S(1)} all-gather(bf16[64,512]{1,0:T(8,128)(2,1)} %param.9), channel_id=1, replica_groups=mesh['gx'=8,'gz'=4] {'gx'}, dimensions={0}, use_global_device_ids=true | all-gather | bytes 589824 | tf_op jit(solution)/shard_map/all_gather | solution.py:72
  56.9 53.9 %all_to_all.141 = bf16[2,16,128,512]{2,1,0,3:T(8,128)(2,1)} all-to-all(bf16[2,16,128,512]{2,1,0,3:T(8,128)(2,1)} %copy.51), channel_id=1, replica_groups=mesh['gx'=8,'gz'=4] {'gz'}, dimensions={3} | all-to-all | bytes 8388608 | tf_op jit(solution)/shard_map/all_to_all | solution.py:24
  125.8 51.6 %all_to_all.142 = bf16[2,64,128,128]{3,2,0,1:T(8,128)(2,1)} all-to-all(bf16[2,64,128,128]{3,2,0,1:T(8,128)(2,1)S(1)} %copy.53), channel_id=1, replica_groups=mesh['gx'=8,'gz'=4] {'gz'}, dimensions={1} | all-to-all | bytes 8388608 | tf_op jit(solution)/shard_map/all_to_all | solution.py:25
  191.7 117.5 %all-to-all-done.2 = bf16[2,16,128,512]{2,1,0,3:T(8,128)(2,1)} async-done(((bf16[2,16,128,512]{2,1,0,3:T(8,128)(2,1)}), bf16[2,16,128,512]{2,1,0,3:T(8,128)(2,1)}, u32[]{:S(2)}, u32[]{:S(2)}) %all-to-all-start.2) | async-done | bytes 4194336 | tf_op jit(solution)/shard_map/all_to_all | solution.py:29
  323.4 9.5 convert_bitcast_fusion.2
  332.8 12.9 copy.59
  345.7 10.5 reshape.38
  363.3 90.1 %all-to-all-done.3 = bf16[8,2,131072]{2,1,0:T(2,128)(2,1)} async-done(((bf16[8,2,131072]{2,1,0:T(2,128)(2,1)}), bf16[8,2,131072]{2,1,0:T(2,128)(2,1)}, u32[]{:S(2)}, u32[]{:S(2)}) %all-to-all-start.3) | async-done | bytes 4194336 | tf_op jit(solution)/shard_map/all_to_all | solution.py:30
  453.4 10.3 reshape.39
  463.7 9.3 copy.97
  506.6 11.2 fusion.10
  517.8 122.0 %add_add_fusion = (bf16[16,128,512]{1,2,0:T(8,128)(2,1)S(1)}, f32[16,128,512]{1,2,0:T(8,128)}) fusion(f32[16,128,512]{1,2,0:T(8,128)} %bitcast.166, f32[18,130,514]{1,2,0:T(8,128)} %fusion.10, f32[]{:T(128)} %bitcast.79, f32[]{:T(128)} %bitcast.78, f32[]{:T(128)} %bitcast.77, f32[]{:T(128)} %bitcast.76, f32[]{:T(128)} %bitcast.75, f32[]{:T(128)} %bitcast.74, ...), kind=kLoop, calls=%fused_computation.148 | loop fusion | flops 114294784 | bytes 123732184 | tf_op jit(solution)/shard_map/add | solution.py:66
  645.7 35.0 %all-reduce.4.cloned.1.call-done = f32[2,128,512]{2,1,0:T(8,128)} async-done(((f32[2,128,512]{2,1,0:T(8,128)}), f32[2,128,512]{2,1,0:T(8,128)}) %all-reduce.4.cloned.1.call-update) | async-done | bytes 524304 | tf_op jit(solution)/shard_map/psum | solution.py:111
  723.4 22.6 %fusion.1 = f32[2,18,130,514]{2,3,1,0:T(8,128)S(1)} fusion(bf16[2,1,130,512]{2,3,1,0:T(8,128)(2,1)} %collective-permute-done.7, bf16[2,1,130,512]{2,3,1,0:T(8,128)(2,1)S(1)} %collective-permute-done.6, bf16[2,16,1,512]{2,3,1,0:T(8,128)(2,1)} %copy.73, bf16[2,16,1,512]{2,3,1,0:T(8,128)(2,1)} %copy.72, bf16[1,16,128,512]{2,3,1,0:T(8,128)(2,1)S(1)} %multiply_convert_fusion, ...), kind=kLoop, calls=%fused_computation.8 | loop fusion | flops 50515920 | bytes 14414400 | tf_op jit(solution)/shard_map/convert_element_type | solution.py:119
  752.9 196.9 %fusion.84 = bf16[1,16,128,512]{2,3,1,0:T(8,128)(2,1)S(1)} fusion(f32[18,130,514]{1,2,0:T(8,128)} %get-tuple-element.5, f32[]{:T(128)} %bitcast.79, f32[]{:T(128)} %bitcast.78, f32[]{:T(128)} %bitcast.77, f32[]{:T(128)} %bitcast.76, f32[]{:T(128)} %bitcast.75, f32[]{:T(128)} %bitcast.74, f32[]{:T(128)} %bitcast.73, f32[]{:T(128)} %bitcast.72, f32[]{:T(128)} %bitcast.71, ...), kind=kLoop, calls=%fused_computation.161 | loop fusion | flops 115343360 | bytes 228852000 | tf_op jit(solution)/shard_map/stack | solution.py:124
  952.9 97.5 %all_to_all.143 = bf16[2,16,128,512]{2,1,0,3:T(8,128)(2,1)S(1)} all-to-all(bf16[2,16,128,512]{2,1,0,3:T(8,128)(2,1)S(1)} %copy.74), channel_id=1, replica_groups=mesh['gx'=8,'gz'=4] {'gx'}, dimensions={3} | all-to-all | bytes 8388608 | tf_op jit(solution)/shard_map/all_to_all | solution.py:29
  1071.0 12.9 copy.77
  1083.9 10.5 reshape.40
  1094.3 97.9 %all_to_all.144 = bf16[8,2,131072]{2,1,0:T(2,128)(2,1)} all-to-all(bf16[8,2,131072]{2,1,0:T(2,128)(2,1)} %reshape.40), channel_id=1, replica_groups=mesh['gx'=8,'gz'=4] {'gx'}, dimensions={0} | all-to-all | bytes 8388608 | tf_op jit(solution)/shard_map/all_to_all | solution.py:30
  1192.2 10.3 reshape.41
  1202.5 14.8 %copy.101 = bf16[2,16,128,8,64]{2,1,0,4,3:T(8,128)(2,1)} copy(bf16[2,16,128,8,64]{4,1,0,2,3:T(8,128)(2,1)} %bitcast.171) | data formatting | bytes 8388608 | tf_op jit(solution)/shard_map/all_to_all | solution.py:30
  1217.2 54.1 %all_to_all.145 = bf16[2,16,128,512]{2,1,0,3:T(8,128)(2,1)} all-to-all(bf16[2,16,128,512]{2,1,0,3:T(8,128)(2,1)} %bitcast.173), channel_id=1, replica_groups=mesh['gx'=8,'gz'=4] {'gz'}, dimensions={3} | all-to-all | bytes 8388608 | tf_op jit(solution)/shard_map/all_to_all | solution.py:24
  1286.5 50.7 %all_to_all.146 = bf16[2,64,128,128]{3,2,0,1:T(8,128)(2,1)S(1)} all-to-all(bf16[2,64,128,128]{3,2,0,1:T(8,128)(2,1)S(1)} %copy.84), channel_id=1, replica_groups=mesh['gx'=8,'gz'=4] {'gz'}, dimensions={1} | all-to-all | bytes 8388608 | tf_op jit(solution)/shard_map/all_to_all | solution.py:25
  1350.4 10.4 convolution_add_fusion
  (103 shorter events, 207.8 us)
Async XLA Ops:
  7.2 112.5 %copy-start = (bf16[64,64]{1,0:T(8,128)(2,1)S(1)}, bf16[64,64]{1,0:T(8,128)(2,1)}, u32[]{:S(2)}) copy-start(bf16[64,64]{1,0:T(8,128)(2,1)} %param.10) | copy-start | bytes 24580
  40.4 0.8 copy-start.7
  185.3 123.9 %all-to-all-start.2 = ((bf16[2,16,128,512]{2,1,0,3:T(8,128)(2,1)}), bf16[2,16,128,512]{2,1,0,3:T(8,128)(2,1)}, u32[]{:S(2)}, u32[]{:S(2)}) async-start(bf16[2,16,128,512]{2,1,0,3:T(8,128)(2,1)} %bitcast.174), calls=%async_computation.2 | async-start | bytes 8388608 | tf_op jit(solution)/shard_map/all_to_all | solution.py:29
  191.0 132.4 %all-gather.2.cloned.1.call-start = ((), (), s32[]{:S(2)}) async-start(), calls=%async_computation.8 | async-start | bytes 2359296 | tf_op jit(solution)/shard_map/all_gather | solution.py:71
  356.2 4.9 copy-start.11
  356.2 97.2 %all-to-all-start.3 = ((bf16[8,2,131072]{2,1,0:T(2,128)(2,1)}), bf16[8,2,131072]{2,1,0:T(2,128)(2,1)}, u32[]{:S(2)}, u32[]{:S(2)}) async-start(bf16[8,2,131072]{2,1,0:T(2,128)(2,1)} %reshape.38), calls=%async_computation.3 | async-start | bytes 8388608 | tf_op jit(solution)/shard_map/all_to_all | solution.py:30
  360.9 319.8 %all-reduce.4.cloned.1.call-start = ((), (), s32[]{:S(2)}) async-start(), calls=%async_computation.9 | async-start | bytes 1048576 | tf_op jit(solution)/shard_map/psum | solution.py:111
  485.1 11.4 collective-permute-start.1
  486.4 8.3 collective-permute-start
  498.3 4.3 copy-start.5
  498.3 4.8 copy-start.4
  499.9 6.0 collective-permute-start.2
  501.4 4.6 collective-permute-start.3
  503.1 2.8 copy-start.2
  503.2 3.4 copy-start.3
  639.8 41.0 %copy-start.10 = (f32[2,128,512]{2,1,0:T(8,128)S(1)}, f32[2,128,512]{2,1,0:T(8,128)}, u32[]{:S(2)}) copy-start(f32[2,128,512]{2,1,0:T(8,128)} %param.7) | copy-start | bytes 1572868
  689.7 4.5 copy-start.1
  697.9 8.7 collective-permute-start.4
  705.3 5.8 collective-permute-start.5
  717.2 3.0 collective-permute-start.6
  718.5 4.9 collective-permute-start.7
  752.9 196.9 %copy-start.6 = (bf16[1,16,128,512]{2,3,1,0:T(8,128)(2,1)S(1)}, bf16[1,16,128,512]{2,3,1,0:T(8,128)(2,1)}, u32[]{:S(2)}) copy-start(bf16[1,16,128,512]{2,3,1,0:T(8,128)(2,1)} %get-tuple-element.11) | copy-start | bytes 6291460
  1055.1 7.4 copy-start.12
  1343.1 7.3 copy-start.8
  (1 other events, 0.8 us)
Sparse Core Ops, SparseCore 0:
  193.9 102.6 all-gather.1
  645.8 34.8 all-reduce.3
where the time goes:
time: 1380 us; the launch traced here: 1370 us
  blocking collectives  439 us (32%)
  other arithmetic  376 us (27%)
  waiting for transfers between devices  248 us (18%)
  local copies, waits for them, and re-layouts  219 us (16%)
  matrix products  45.4 us (3%)
  starting transfers between devices  26.9 us (2%)
  between operations  14.6 us (1%)
    another operation x2, other arithmetic, local(): jnp.stack([back_g + spread_back, back_m * growth]).astype(jnp.bfloat16)  197 us
    add x1, other arithmetic, coupling_forward(): return (scale, growth, magnetic_f * growth + pre_shift)  122 us
    all_to_all x1, waiting for transfers between devices, across_lines(): lax.all_to_all(values, 'gx', split_axis=3, concat_axis=2, tiled=True)  117 us
    all_to_all x2, blocking collectives, depth_lines(): lax.all_to_all(values, 'gz', split_axis=3, concat_axis=1, tiled=True)  108 us
    all_to_all x2, blocking collectives, depth_lines(): lax.all_to_all(local_step(turned), 'gz', split_axis=1, concat_axis=3, til...  102 us
    all_to_all x1, blocking collectives, across_lines(): lax.all_to_all(local_step(turned), 'gx', split_axis=2, concat_axis=3, til...  97.9 us
    all_to_all x1, blocking collectives, across_lines(): lax.all_to_all(values, 'gx', split_axis=3, concat_axis=2, tiled=True)  97.5 us
    all_to_all x1, waiting for transfers between devices, across_lines(): lax.all_to_all(local_step(turned), 'gx', split_axis=2, concat_axis=3, til...  90.1 us
  transfers between devices with their start and end apart: 12, of which 6 were waited for; matrix products, arithmetic and copies ran while one was open for 2% of the time, Pallas kernels for 0%

commit v1 on v0

--- a/solution.py
+++ b/solution.py
@@ -5,6 +5,34 @@
 from jax.sharding import PartitionSpec as P
 
 NZ = 64
+
+
+def guide_types(x_local):
+    b_now, state_next, view_out = (lax.axis_size("gx"), lax.axis_index("gx"), x_local.shape[0])
+    shelf = []
+    for u, ii in enumerate(x_local.shape):
+        shelf.append(ii * b_now if u == 0 else ii)
+    all_rows = lax.dynamic_update_slice_in_dim(
+        jnp.zeros(shelf, x_local.dtype), x_local, state_next * view_out, axis=0
+    )
+    part_next = item_now = x_local
+    for dev_j in tuple(range(1, b_now // 2 + 1)):
+        store = []
+        for u in tuple(range(b_now)):
+            store.append((u, (u + 1) % b_now))
+        part_next = lax.ppermute(part_next, "gx", store)
+        all_rows = lax.dynamic_update_slice_in_dim(
+            all_rows, part_next, (state_next - dev_j) % b_now * view_out, axis=0
+        )
+        if 2 * dev_j < b_now:
+            rows = []
+            for u in [*range(b_now)]:
+                rows.append((u, (u - 1) % b_now))
+            item_now = lax.ppermute(item_now, "gx", rows)
+            all_rows = lax.dynamic_update_slice_in_dim(
+                all_rows, item_now, (state_next + dev_j) % b_now * view_out, axis=0
+            )
+    return all_rows
 
 
 def padded_2(x, sides, width):
@@ -67,10 +95,7 @@
 
 
 def local(whitened, observed, lower_x, lower_y, lower_z, coupling_kernel):
-    factor_x, factor_y = (
-        lax.all_gather(lower_x, "gx", axis=0, tiled=True),
-        lax.all_gather(lower_y, "gx", axis=0, tiled=True),
-    )
+    factor_x, factor_y = (lax.all_gather(lower_x, "gx", axis=0, tiled=True), guide_types(lower_y))
 
     def apply_depth(values):
         return jnp.einsum(

time: 1380 us -> 1370 us (level)
  blocking collectives: 439 us -> 403 us
  waiting for transfers between devices: 248 us -> 265 us
  starting transfers between devices: 26.9 us -> 41.9 us
    all_gather x1 -> x0, blocking collectives: 33.2 us -> none  [local(): lax.all_gather(lower_y, 'gx', axis=0, tiled=True)]
    ppermute x0 -> x7, waiting for transfers between devices: none -> 17 us  [the longest x4 13.9 us: guide_types(): part_next = lax.ppermute(part_next, 'gx', store)]
    ppermute x0 -> x7, starting transfers between devices: none -> 16.1 us  [the longest x3 16.1 us: guide_types(): item_now = lax.ppermute(item_now, 'gx', rows)]
  transfers between devices with their start and end apart: 12 -> 19, of which waited for: 6 -> 11; matrix products, arithmetic and copies ran while one was open for 2% -> 2% of each run, Pallas kernels for 0% -> 0%
where the time goes in v1:
time: 1370 us; the launch traced here: 1360 us
  blocking collectives  403 us (29%)
  other arithmetic  375 us (27%)
  waiting for transfers between devices  265 us (19%)
  local copies, waits for them, and re-layouts  214 us (16%)
  matrix products  43.8 us (3%)
  starting transfers between devices  41.9 us (3%)
  between operations  14.7 us (1%)
    another operation x2, other arithmetic, local(): jnp.stack([back_g + spread_back, back_m * growth]).astype(jnp.bfloat16)  197 us
    add x1, other arithmetic, coupling_forward(): return (scale, growth, magnetic_f * growth + pre_shift)  122 us
    all_to_all x1, waiting for transfers between devices, across_lines(): lax.all_to_all(values, 'gx', split_axis=3, concat_axis=2, tiled=True)  118 us
    all_to_all x2, blocking collectives, depth_lines(): lax.all_to_all(values, 'gz', split_axis=3, concat_axis=1, tiled=True)  106 us
    all_to_all x2, blocking collectives, depth_lines(): lax.all_to_all(local_step(turned), 'gz', split_axis=1, concat_axis=3, til...  102 us
    all_to_all x1, blocking collectives, across_lines(): lax.all_to_all(local_step(turned), 'gx', split_axis=2, concat_axis=3, til...  97.9 us
    all_to_all x1, blocking collectives, across_lines(): lax.all_to_all(values, 'gx', split_axis=3, concat_axis=2, tiled=True)  97.5 us
    all_to_all x1, waiting for transfers between devices, across_lines(): lax.all_to_all(local_step(turned), 'gx', split_axis=2, concat_axis=3, til...  90.1 us
  transfers between devices with their start and end apart: 19, of which 11 were waited for; matrix products, arithmetic and copies ran while one was open for 2% of the time, Pallas kernels for 0%

profile of v1, /device:TPU:0, one launch (start us, length us, event | category | flops | bytes accessed | tf_op | source)
XLA Modules:
  0.0 1357.9 jit_solution(6025576722862472405)
XLA Ops:
  50.3 51.6 %all_to_all.141 = bf16[2,16,128,512]{2,1,0,3:T(8,128)(2,1)} all-to-all(bf16[2,16,128,512]{2,1,0,3:T(8,128)(2,1)S(1)} %copy.51), channel_id=1, replica_groups=mesh['gx'=8,'gz'=4] {'gz'}, dimensions={3} | all-to-all | bytes 8388608 | tf_op jit(solution)/shard_map/all_to_all | solution.py:52
  101.9 9.0 copy.52
  117.0 51.6 %all_to_all.142 = bf16[2,64,128,128]{3,2,0,1:T(8,128)(2,1)} all-to-all(bf16[2,64,128,128]{3,2,0,1:T(8,128)(2,1)S(1)} %copy.53), channel_id=1, replica_groups=mesh['gx'=8,'gz'=4] {'gz'}, dimensions={1} | all-to-all | bytes 8388608 | tf_op jit(solution)/shard_map/all_to_all | solution.py:53
  181.7 117.6 %all-to-all-done.2 = bf16[2,16,128,512]{2,1,0,3:T(8,128)(2,1)} async-done(((bf16[2,16,128,512]{2,1,0,3:T(8,128)(2,1)}), bf16[2,16,128,512]{2,1,0,3:T(8,128)(2,1)}, u32[]{:S(2)}, u32[]{:S(2)}) %all-to-all-start.2) | async-done | bytes 4194336 | tf_op jit(solution)/shard_map/all_to_all | solution.py:57
  313.5 9.4 convert_bitcast_fusion.2
  323.0 12.9 copy.59
  335.9 10.5 reshape.38
  353.5 90.1 %all-to-all-done.3 = bf16[8,2,131072]{2,1,0:T(2,128)(2,1)} async-done(((bf16[8,2,131072]{2,1,0:T(2,128)(2,1)}), bf16[8,2,131072]{2,1,0:T(2,128)(2,1)}, u32[]{:S(2)}, u32[]{:S(2)}) %all-to-all-start.3) | async-done | bytes 4194336 | tf_op jit(solution)/shard_map/all_to_all | solution.py:58
  443.6 10.3 reshape.39
  453.9 9.3 copy.97
  496.7 11.2 fusion.10
  507.9 121.9 %add_add_fusion = (bf16[16,128,512]{1,2,0:T(8,128)(2,1)S(1)}, f32[16,128,512]{1,2,0:T(8,128)}) fusion(f32[16,128,512]{1,2,0:T(8,128)} %bitcast.168, f32[18,130,514]{1,2,0:T(8,128)} %fusion.10, f32[]{:T(128)} %bitcast.80, f32[]{:T(128)} %bitcast.79, f32[]{:T(128)} %bitcast.78, f32[]{:T(128)} %bitcast.77, f32[]{:T(128)} %bitcast.76, f32[]{:T(128)} %bitcast.75, ...), kind=kLoop, calls=%fused_computation.148 | loop fusion | flops 114294784 | bytes 123732184 | tf_op jit(solution)/shard_map/add | solution.py:94
  635.8 35.3 %all-reduce.4.cloned.1.call-done = f32[2,128,512]{2,1,0:T(8,128)} async-done(((f32[2,128,512]{2,1,0:T(8,128)}), f32[2,128,512]{2,1,0:T(8,128)}) %all-reduce.4.cloned.1.call-update) | async-done | bytes 524304 | tf_op jit(solution)/shard_map/psum | solution.py:136
  713.7 22.6 %fusion.1 = f32[2,18,130,514]{2,3,1,0:T(8,128)S(1)} fusion(bf16[2,1,130,512]{2,3,1,0:T(8,128)(2,1)} %collective-permute-done.14, bf16[2,1,130,512]{2,3,1,0:T(8,128)(2,1)S(1)} %collective-permute-done.13, bf16[2,16,1,512]{2,3,1,0:T(8,128)(2,1)} %copy.73, bf16[2,16,1,512]{2,3,1,0:T(8,128)(2,1)} %copy.72, bf16[1,16,128,512]{2,3,1,0:T(8,128)(2,1)S(1)} %multiply_convert_fusion, ...), kind=kLoop, calls=%fused_computation.8 | loop fusion | flops 50515920 | bytes 14414400 | tf_op jit(solution)/shard_map/convert_element_type | solution.py:144
  743.3 196.6 %fusion.83 = bf16[1,16,128,512]{2,3,1,0:T(8,128)(2,1)S(1)} fusion(f32[18,130,514]{1,2,0:T(8,128)} %get-tuple-element.5, f32[]{:T(128)} %bitcast.80, f32[]{:T(128)} %bitcast.79, f32[]{:T(128)} %bitcast.78, f32[]{:T(128)} %bitcast.77, f32[]{:T(128)} %bitcast.76, f32[]{:T(128)} %bitcast.75, f32[]{:T(128)} %bitcast.74, f32[]{:T(128)} %bitcast.73, f32[]{:T(128)} %bitcast.72, ...), kind=kLoop, calls=%fused_computation.161 | loop fusion | flops 115343360 | bytes 228852000 | tf_op jit(solution)/shard_map/stack | solution.py:149
  943.0 97.5 %all_to_all.143 = bf16[2,16,128,512]{2,1,0,3:T(8,128)(2,1)S(1)} all-to-all(bf16[2,16,128,512]{2,1,0,3:T(8,128)(2,1)S(1)} %copy.74), channel_id=1, replica_groups=mesh['gx'=8,'gz'=4] {'gx'}, dimensions={3} | all-to-all | bytes 8388608 | tf_op jit(solution)/shard_map/all_to_all | solution.py:57
  1061.0 12.9 copy.77
  1073.9 10.5 reshape.40
  1084.4 97.9 %all_to_all.144 = bf16[8,2,131072]{2,1,0:T(2,128)(2,1)} all-to-all(bf16[8,2,131072]{2,1,0:T(2,128)(2,1)} %reshape.40), channel_id=1, replica_groups=mesh['gx'=8,'gz'=4] {'gx'}, dimensions={0} | all-to-all | bytes 8388608 | tf_op jit(solution)/shard_map/all_to_all | solution.py:58
  1182.2 10.3 reshape.41
  1192.5 14.8 %copy.101 = bf16[2,16,128,8,64]{2,1,0,4,3:T(8,128)(2,1)} copy(bf16[2,16,128,8,64]{4,1,0,2,3:T(8,128)(2,1)} %bitcast.173) | data formatting | bytes 8388608 | tf_op jit(solution)/shard_map/all_to_all | solution.py:58
  1207.3 54.1 %all_to_all.145 = bf16[2,16,128,512]{2,1,0,3:T(8,128)(2,1)} all-to-all(bf16[2,16,128,512]{2,1,0,3:T(8,128)(2,1)} %bitcast.175), channel_id=1, replica_groups=mesh['gx'=8,'gz'=4] {'gz'}, dimensions={3} | all-to-all | bytes 8388608 | tf_op jit(solution)/shard_map/all_to_all | solution.py:52
  1276.5 50.7 %all_to_all.146 = bf16[2,64,128,128]{3,2,0,1:T(8,128)(2,1)S(1)} all-to-all(bf16[2,64,128,128]{3,2,0,1:T(8,128)(2,1)S(1)} %copy.84), channel_id=1, replica_groups=mesh['gx'=8,'gz'=4] {'gz'}, dimensions={1} | all-to-all | bytes 8388608 | tf_op jit(solution)/shard_map/all_to_all | solution.py:53
  1340.4 10.4 convolution_add_fusion
  (125 shorter events, 224.2 us)
Async XLA Ops:
  7.2 103.7 %copy-start = (bf16[64,64]{1,0:T(8,128)(2,1)S(1)}, bf16[64,64]{1,0:T(8,128)(2,1)}, u32[]{:S(2)}) copy-start(bf16[64,64]{1,0:T(8,128)(2,1)} %param.10) | copy-start | bytes 24580
  7.2 8.3 collective-permute-start.1
  13.2 7.2 collective-permute-start
  15.5 6.9 collective-permute-start.3
  20.4 7.0 collective-permute-start.2
  22.3 12.1 collective-permute-start.5
  27.4 7.0 collective-permute-start.4
  34.4 7.0 collective-permute-start.6
  176.4 122.9 %all-to-all-start.2 = ((bf16[2,16,128,512]{2,1,0,3:T(8,128)(2,1)}), bf16[2,16,128,512]{2,1,0,3:T(8,128)(2,1)}, u32[]{:S(2)}, u32[]{:S(2)}) async-start(bf16[2,16,128,512]{2,1,0,3:T(8,128)(2,1)} %bitcast.176), calls=%async_computation.2 | async-start | bytes 8388608 | tf_op jit(solution)/shard_map/all_to_all | solution.py:57
  181.0 132.6 %all-gather.2.cloned.1.call-start = ((), (), s32[]{:S(2)}) async-start(), calls=%async_computation.8 | async-start | bytes 2359296 | tf_op jit(solution)/shard_map/all_gather | solution.py:98
  346.4 97.2 %all-to-all-start.3 = ((bf16[8,2,131072]{2,1,0:T(2,128)(2,1)}), bf16[8,2,131072]{2,1,0:T(2,128)(2,1)}, u32[]{:S(2)}, u32[]{:S(2)}) async-start(bf16[8,2,131072]{2,1,0:T(2,128)(2,1)} %reshape.38), calls=%async_computation.3 | async-start | bytes 8388608 | tf_op jit(solution)/shard_map/all_to_all | solution.py:58
  351.1 320.0 %all-reduce.4.cloned.1.call-start = ((), (), s32[]{:S(2)}) async-start(), calls=%async_computation.9 | async-start | bytes 1048576 | tf_op jit(solution)/shard_map/psum | solution.py:136
  475.3 11.4 collective-permute-start.8
  476.6 8.3 collective-permute-start.7
  490.1 6.0 collective-permute-start.9
  491.5 4.7 collective-permute-start.10
  629.9 41.2 %copy-start.10 = (f32[2,128,512]{2,1,0:T(8,128)S(1)}, f32[2,128,512]{2,1,0:T(8,128)}, u32[]{:S(2)}) copy-start(f32[2,128,512]{2,1,0:T(8,128)} %param.7) | copy-start | bytes 1572868
  688.2 8.7 collective-permute-start.11
  695.6 5.8 collective-permute-start.12
  707.5 3.0 collective-permute-start.13
  708.9 4.9 collective-permute-start.14
  743.3 196.6 %copy-start.6 = (bf16[1,16,128,512]{2,3,1,0:T(8,128)(2,1)S(1)}, bf16[1,16,128,512]{2,3,1,0:T(8,128)(2,1)}, u32[]{:S(2)}) copy-start(bf16[1,16,128,512]{2,3,1,0:T(8,128)(2,1)} %get-tuple-element.11) | copy-start | bytes 6291460
  1045.1 7.5 copy-start.12
  1333.2 7.3 copy-start.8
  (8 other events, 31.8 us)
Sparse Core Ops, SparseCore 0:
  183.9 102.8 all-gather.1
  635.9 35.1 all-reduce.3
